TPU v7x, 32 devices: a whole 2x2x4 slice. The times are simulated.
32 devices in a mesh: grp: 2 (over x), req: 16 (over z, y, core).
Axes of the slice: x: 2, y: 2, z: 4, core: 2. Of those that a mesh axis runs over, the one named last changes fastest.
Arguments:
- xbc: bfloat16 [4096, 9216], P(('grp', 'req')), parts along dimension 0, may hold values from -6 to 6
- dt_raw: float32 [4096, 128], P(('grp', 'req')), parts along dimension 0, may hold values from -6 to 6
- conv_weight: float32 [4, 9216], replicated, may hold values from -3 to 3
- conv_bias: float32 [9216], replicated, may hold values from -3 to 3
- dt_bias: float32 [128], replicated, may hold values from -1 to 1
- a_log: float32 [128], replicated, may hold values from -6 to -2.5
- d_skip: float32 [128], replicated, may hold values from 0.5 to 1.5
- cache_states: bfloat16 [96, 128, 8192], P(('grp', 'req')), parts along dimension 0, may hold values from -24 to 24
- cache_tails: bfloat16 [96, 3, 9216], P(('grp', 'req')), parts along dimension 0, may hold values from -6 to 6
- hit_owner: int32 [32], P('grp'), parts along dimension 0, may hold values from 0 to 15, as said below
- hit_slot: int32 [32], P('grp'), parts along dimension 0, may hold values from 0 to 2, as said below
- hit_spans: int32 [32], P('grp'), parts along dimension 0, may hold values from 0 to 4
- request_of: int32 [32], P(('grp', 'req')), parts along dimension 0, may hold values from 0 to 15, each once
Outputs:
- y_out: bfloat16 [4096, 8192], P(('grp', 'req')), parts along dimension 0
- final_state: bfloat16 [32, 128, 8192], P(('grp', 'req')), parts along dimension 0
There are 2 independent parts, one for each index of `grp`. A program takes and returns all parts, laid end to end along the dimension named above; an argument that names none is the same for every part. Nothing has to cross between parts.
Inputs may be any that keep to these rules, and one draw needn't show every extreme that they name: `hit_owner`: owners are skewed: some devices hold the prefixes of several requests, others of none. `hit_slot`: all requests that name the same owner device name the same slot of it. `request_of`: each request stands on exactly one device.
All inputs are finite; a program needn't handle non-finite values.
Results may differ from a plain program's by a relative error of at most 0.0039.
Values may be sent and summed in bfloat16 or wider, within the bound.
A program may use at most 128 MiB of HBM per device.

v0:
```python
import jax
import jax.numpy as jnp
from jax import lax
from jax.sharding import PartitionSpec as P

HEADS = 128
HEAD_DIM = 64
GROUPS = 4
NST = 128
INNER = 8192


def convolve(xrows, tail, conv_weight, conv_bias):
    rows = xrows.shape[0]
    taps = conv_weight.shape[0]
    extended = jnp.concatenate([tail, xrows], axis=0).astype(jnp.float32)
    conv = jnp.zeros((rows, xrows.shape[1]), jnp.float32) + conv_bias[None, :]
    for k in range(taps):
        conv = conv + conv_weight[k][None, :] * extended[k : k + rows]
    return jax.nn.silu(conv).astype(jnp.bfloat16)


def local_part(conv_out, dt_rows, dt_bias, a_log, d_skip):
    rows = conv_out.shape[0]
    per_group = HEADS // GROUPS
    inputs = conv_out[:, :INNER].reshape(rows, GROUPS, per_group, HEAD_DIM)
    b_part = conv_out[:, INNER : INNER + GROUPS * NST].reshape(rows, GROUPS, NST)
    c_part = conv_out[:, INNER + GROUPS * NST :].reshape(rows, GROUPS, NST)
    step = jax.nn.softplus(dt_rows + dt_bias[None, :])
    cum = jnp.cumsum(step * (-jnp.exp(a_log))[None, :], axis=0)
    scores = jnp.einsum("tgn,sgn->gts", c_part, b_part, preferred_element_type=jnp.float32)
    diff = cum.T[:, :, None] - cum.T[:, None, :]
    causal = lax.broadcasted_iota(jnp.int32, (rows, rows), 0) >= lax.broadcasted_iota(
        jnp.int32, (rows, rows), 1
    )
    decay = jnp.where(causal[None], jnp.exp(jnp.minimum(diff, 0.0)), 0.0)
    mixing = (
        scores[:, None]
        * decay.reshape(GROUPS, per_group, rows, rows)
        * step.T.reshape(GROUPS, per_group, 1, rows)
    ).astype(jnp.bfloat16)
    y_intra = jnp.einsum("gjts,sgjp->tgjp", mixing, inputs, preferred_element_type=jnp.float32)
    y_local = y_intra + d_skip.reshape(1, GROUPS, per_group, 1) * inputs.astype(jnp.float32)
    last = cum[rows - 1]
    carried = (
        (jnp.exp(last[None, :] - cum) * step).reshape(rows, GROUPS, per_group, 1)
        * inputs.astype(jnp.float32)
    ).astype(jnp.bfloat16)
    fresh = jnp.einsum("sgn,sgjp->ngjp", b_part, carried, preferred_element_type=jnp.float32)
    return (y_local, fresh, c_part, cum)


def state_part(start, c_part, cum):
    rows = c_part.shape[0]
    per_group = HEADS // GROUPS
    start_view = start.reshape(NST, GROUPS, per_group, HEAD_DIM)
    y_state = jnp.einsum("tgn,ngjp->tgjp", c_part, start_view, preferred_element_type=jnp.float32)
    y_state = y_state * jnp.exp(cum).reshape(rows, GROUPS, per_group, 1)
    kept = jnp.exp(cum[rows - 1]).reshape(1, GROUPS, per_group, 1) * start_view.astype(jnp.float32)
    return (y_state, kept)


def local(
    xbc,
    dt_raw,
    conv_weight,
    conv_bias,
    dt_bias,
    a_log,
    d_skip,
    cache_states,
    cache_tails,
    hit_owner,
    hit_slot,
    hit_spans,
    request_of,
):
    slots = cache_states.shape[0]
    every_request = lax.all_gather(request_of, "req", axis=0, tiled=True)
    mine = request_of[0]
    own_row = hit_owner[mine] * slots + hit_slot[mine]
    live = hit_spans[mine] > 0
    device = lax.axis_index("req")
    served = jnp.max(jnp.where(hit_owner == device, hit_slot, 0))
    send_states = lax.dynamic_slice_in_dim(cache_states, served, 1, 0)
    wanted_rows = hit_owner[every_request]
    every_tail = lax.all_gather(cache_tails, "req", axis=0, tiled=True)
    tail = lax.dynamic_index_in_dim(every_tail, own_row, 0, keepdims=False)
    state_parts = lax.all_to_all(send_states, "req", split_axis=2, concat_axis=0, tiled=True)
    state_chosen = jnp.take(state_parts, wanted_rows, axis=0)
    start = lax.all_to_all(state_chosen, "req", split_axis=0, concat_axis=2, tiled=True)[0]
    tail = jnp.where(live, tail, jnp.zeros_like(tail))
    start = jnp.where(live, start, jnp.zeros_like(start))
    conv_out = convolve(xbc, tail, conv_weight, conv_bias)
    y_local, fresh, c_part, cum = local_part(conv_out, dt_raw, dt_bias, a_log, d_skip)
    y_state, kept = state_part(start, c_part, cum)
    rows = xbc.shape[0]
    y_out = (y_local + y_state).reshape(rows, INNER).astype(jnp.bfloat16)
    final_state = (kept + fresh).reshape(1, NST, INNER).astype(jnp.bfloat16)
    return (y_out, final_state)


def solution(mesh):
    in_specs = (
        P(("grp", "req"), None),
        P(("grp", "req"), None),
        P(),
        P(),
        P(),
        P(),
        P(),
        P(("grp", "req"), None, None),
        P(("grp", "req"), None, None),
        P("grp"),
        P("grp"),
        P("grp"),
        P(("grp", "req")),
    )
    out_specs = (P(("grp", "req"), None), P(("grp", "req"), None, None))
    return jax.shard_map(local, mesh=mesh, in_specs=in_specs, out_specs=out_specs, check_vma=False)
```

profile of v0, /device:TPU:15, one launch (start us, length us, event | category | flops | bytes accessed | tf_op | source)
XLA Modules:
  0.0 240.6 jit_solution(13793065196203515922)
XLA Ops:
  7.2 0.0 all-gather.2.cloned.1.call-start
  7.9 1.2 dynamic-slice
  9.1 0.8 dynamic-update-slice
  9.9 0.0 all-gather.2.cloned.1.call-update
  9.9 7.9 %all-reduce = s32[16]{0:T(128)S(1)} all-reduce(s32[16]{0:T(128)S(1)} %dynamic-update-slice), channel_id=1, replica_groups=mesh['grp'=2,'req'=16] {'req'}, use_global_device_ids=true, to_apply=%add | all-reduce | flops 16 | bytes 128
  17.8 1.3 compare_select_fusion.3
  21.1 1.7 constant_dynamic-slice_fusion
  22.8 6.9 %copy.73 = bf16[1,128,8192]{1,0,2:T(2,128)(2,1)} copy(bf16[1,128,8192]{2,1,0:T(8,128)(2,1)S(1)} %constant_dynamic-slice_fusion) | data formatting | bytes 4194304
  29.7 0.5 broadcast.94
  30.2 45.2 %reduce.4 = bf16[8192,128]{1,0:T(8,128)(2,1)S(1)} reduce(bf16[8192,1,128]{2,1,0:T(2,128)(2,1)} %bitcast.66, bf16[]{:T(256)} %broadcast.94), dimensions={1}, to_apply=%bitcast.55.reduce_sub_computation | reduce | bytes 4194306
  75.4 0.0 copy-start
  75.4 0.0 copy-start.8
  75.4 0.0 copy-start.9
  75.4 2.0 reshape.136
  77.4 9.4 %all-to-all-start = ((bf16[16,2,32768]{2,1,0:T(2,128)(2,1)}), bf16[16,2,32768]{2,1,0:T(2,128)(2,1)}, u32[]{:S(2)}, u32[]{:S(2)}) async-start(bf16[16,2,32768]{2,1,0:T(2,128)(2,1)} %reshape.136), calls=%async_computation | async-start | bytes 4194304 | tf_op jit(solution)/shard_map/all_to_all | solution.py:89
  86.9 0.0 copy-start.4
  86.9 0.0 copy-done
  86.9 0.6 dynamic_slice.17
  87.5 0.0 copy-done.8
  87.5 0.7 dynamic_slice.18
  89.5 0.0 copy-done.9
  89.5 0.7 dynamic_slice.16
  90.1 3.0 %copy.50 = bf16[128,9216]{0,1:T(8,128)(2,1)S(1)} copy(bf16[128,9216]{1,0:T(8,128)(2,1)} %param.13) | data formatting | bytes 4718592 | tf_op args[0]
  93.2 0.7 gather_fusion
  93.8 0.0 copy-done.10
  93.9 0.0 copy-done.3
  93.9 0.0 copy-done.6
  93.9 0.1 broadcast_multiply_fusion
  93.9 0.2 reduce_window_sum.11
  94.1 0.1 exponential_multiply_fusion
  94.2 0.1 copy.60
  94.3 0.1 exp.45
  94.4 0.1 copy.54
  94.5 0.1 copy.53
  94.6 0.1 copy.59
  94.7 0.1 mul.134
  95.5 0.1 fusion.23
  95.7 38.7 %all-to-all-done = bf16[16,2,32768]{2,1,0:T(2,128)(2,1)} async-done(((bf16[16,2,32768]{2,1,0:T(2,128)(2,1)}), bf16[16,2,32768]{2,1,0:T(2,128)(2,1)}, u32[]{:S(2)}, u32[]{:S(2)}) %all-to-all-start) | async-done | bytes 2097184 | tf_op jit(solution)/shard_map/all_to_all | solution.py:89
  134.4 10.4 %reshape.137 = bf16[8192,1,128]{2,1,0:T(2,128)(2,1)} reshape(bf16[16,2,32768]{2,1,0:T(2,128)(2,1)} %all-to-all-done) | data formatting | bytes 4194304
  144.8 3.8 %copy.72 = bf16[1,128,8192]{1,2,0:T(8,128)(2,1)} copy(bf16[1,128,8192]{1,0,2:T(2,128)(2,1)} %bitcast.67) | data formatting | bytes 4194304
  148.6 3.9 %copy.56 = bf16[1,128,16,512]{3,1,2,0:T(8,128)(2,1)} copy(bf16[1,128,16,512]{1,3,2,0:T(8,128)(2,1)} %bitcast.68) | data formatting | bytes 4194304 | tf_op jit(solution)/shard_map/all_to_all | solution.py:89
  152.5 3.6 %gather_fusion.1 = bf16[16,128,512]{2,1,0:T(8,128)(2,1)} fusion(bf16[16,128,512]{2,1,0:T(8,128)(2,1)} %bitcast.69, s32[1024]{0:T(1024)S(1)} %pad_clamp_fusion), kind=kCustom, calls=%fused_computation.1 | custom fusion | bytes 4194368 | tf_op jit(solution)/shard_map/jit(_take)/gather | solution.py:90
  156.1 3.2 %broadcast_select_fusion = bf16[16,128,512]{2,1,0:T(8,128)(2,1)} fusion(bf16[16,128,512]{2,1,0:T(8,128)(2,1)} %gather_fusion.1, pred[16]{0:T(512)(128)(4,1)S(1)} %compare_and_fusion), kind=kLoop, calls=%fused_computation.32 | loop fusion | flops 1048576 | bytes 4194320 | tf_op jit(solution)/shard_map/jit(_take)/select_n | solution.py:90
  159.2 4.9 %all-to-all-start.1 = ((bf16[16,128,512]{2,1,0:T(8,128)(2,1)}), bf16[16,128,512]{2,1,0:T(8,128)(2,1)}, u32[]{:S(2)}, u32[]{:S(2)}) async-start(bf16[16,128,512]{2,1,0:T(8,128)(2,1)} %broadcast_select_fusion), calls=%async_computation.1 | async-start | bytes 4194304 | tf_op jit(solution)/shard_map/all_to_all | solution.py:91
  164.1 0.0 all-gather.2.cloned.1.call-done
  164.2 0.9 constant_dynamic-slice_fusion.1
  165.1 2.0 copy.74
  167.1 1.7 select_bitcast_fusion
  168.8 0.0 copy-start.5
  168.8 1.8 maximum_convert_fusion
  170.7 0.0 copy-done.5
  170.7 11.8 %multiply_convert_fusion.1 = bf16[128,9216]{0,1:T(8,128)(2,1)S(1)} fusion(f32[131,9216]{0,1:T(8,128)S(1)} %maximum_convert_fusion, f32[9216]{0:T(1024)S(1)} %bitcast.85, f32[9216]{0:T(1024)S(1)} %bitcast.86, f32[9216]{0:T(1024)S(1)} %bitcast.84, f32[9216]{0:T(1024)S(1)} %bitcast.83, f32[9216]{0:T(1024)S(1)} %copy-done.5), kind=kLoop, calls=%fused_computation.14 | loop fusion | flops 15335424 | bytes 21417984 | tf_op jit(solution)/shard_map/convert_element_type | solution.py:20
  182.4 0.1 slice.57
  182.6 0.0 copy-start.1
  182.6 0.2 fusion.24
  182.9 1.0 copy-done.1
  183.9 6.0 %fusion.4 = f32[4,32,64,128]{3,2,1,0:T(8,128)} fusion(bf16[128,4,32,64]{0,3,2,1:T(8,128)(2,1)S(1)} %bitcast.70, f32[4,32,128]{2,1,0:T(8,128)S(1)} %bitcast.88, f32[4,32,128]{2,1,0:T(8,128)S(1)} %bitcast.89, f32[4,128,128]{2,1,0:T(8,128)S(1)} %fusion.24, pred[128,128]{1,0:T(8,128)(4,1)S(1)} %iota_compare_fusion), kind=kOutput, calls=%fused_computation.15 | convolution fusion | flops 281018368 | bytes 6701056 | tf_op jit(solution)/shard_map/gjts,sgjp->tgjp/dot_general | solution.py:42
  189.9 21.7 %all-to-all-done.1 = bf16[16,128,512]{2,1,0:T(8,128)(2,1)} async-done(((bf16[16,128,512]{2,1,0:T(8,128)(2,1)}), bf16[16,128,512]{2,1,0:T(8,128)(2,1)}, u32[]{:S(2)}, u32[]{:S(2)}) %all-to-all-start.1) | async-done | bytes 2097184 | tf_op jit(solution)/shard_map/all_to_all | solution.py:91
  211.7 1.7 select_bitcast_fusion.1
  213.4 2.4 copy.57
  215.8 4.7 %fusion.9 = bf16[128,4,32,64]{0,3,2,1:T(8,128)(2,1)} fusion(bf16[128,4,32,64]{0,3,2,1:T(8,128)(2,1)} %bitcast.73, bf16[128,4,128,1]{0,2,3,1:T(8,128)(2,1)S(1)} %bitcast.81, bf16[128,4,32,64]{0,3,2,1:T(8,128)(2,1)} %bitcast.71, f32[128,4,32]{0,2,1:T(8,128)S(1)} %bitcast.87, f32[4,32]{1,0:T(4,128)S(1)} %exp.45), kind=kOutput, calls=%fused_computation.21 | convolution fusion | flops 275775488 | bytes 6488576 | tf_op jit(solution)/shard_map/sgn,sgjp->ngjp/dot_general | solution.py:49
  220.5 4.1 %copy.63 = bf16[1,128,8192]{2,1,0:T(8,128)(2,1)} copy(bf16[1,128,8192]{1,2,0:T(8,128)(2,1)} %bitcast.76) | data formatting | bytes 4194304
  224.5 5.2 %fusion.7 = bf16[128,4,32,64]{0,3,2,1:T(8,128)(2,1)} fusion(bf16[128,4,32,64]{0,3,2,1:T(8,128)(2,1)S(1)} %bitcast.72, f32[4,32,64,128]{3,2,1,0:T(8,128)} %fusion.4, bf16[128,4,32,64]{0,3,2,1:T(8,128)(2,1)} %bitcast.74, bf16[128,4,128,1]{0,2,3,1:T(8,128)(2,1)S(1)} %bitcast.78, f32[128,4,32]{0,2,1:T(8,128)S(1)} %bitcast.82, f32[4,32]{1,0:T(4,128)S(1)} %mul.134), kind=kOutput, calls=%fused_computation.18 | convolution fusion | flops 274726912 | bytes 10682880 | tf_op jit(solution)/shard_map/tgn,ngjp->tgjp/dot_general | solution.py:57
  229.7 4.1 %copy.62 = bf16[128,8192]{1,0:T(8,128)(2,1)} copy(bf16[128,8192]{0,1:T(8,128)(2,1)} %bitcast.75) | data formatting | bytes 4194304
  (17 shorter events, 0.1 us)
Async XLA Ops:
  7.2 157.0 %all-gather.2.cloned.1.call-start = ((), (), s32[]{:S(2)}) async-start(), calls=%async_computation.2 | async-start | bytes 3760128 | tf_op jit(solution)/shard_map/all_gather | solution.py:87
  75.4 11.5 %copy-start = (s32[16]{0:T(128)S(1)}, s32[16]{0:T(128)}, u32[]{:S(2)}) copy-start(s32[16]{0:T(128)} %param.22) | copy-start | bytes 196
  75.4 12.1 %copy-start.8 = (s32[16]{0:T(128)S(1)}, s32[16]{0:T(128)}, u32[]{:S(2)}) copy-start(s32[16]{0:T(128)} %param.23) | copy-start | bytes 196
  75.4 14.1 %copy-start.9 = (s32[16]{0:T(128)S(1)}, s32[16]{0:T(128)}, u32[]{:S(2)}) copy-start(s32[16]{0:T(128)} %param.24) | copy-start | bytes 196
  77.4 16.4 %copy-start.10 = (f32[128]{0:T(128)S(1)}, f32[128]{0:T(128)}, u32[]{:S(2)}) copy-start(f32[128]{0:T(128)} %param.18) | copy-start | bytes 1540
  77.4 16.4 %copy-start.3 = (f32[128,128]{1,0:T(8,128)S(1)}, f32[128,128]{1,0:T(8,128)}, u32[]{:S(2)}) copy-start(f32[128,128]{1,0:T(8,128)} %param.14) | copy-start | bytes 196612
  77.4 16.5 %copy-start.6 = (f32[128]{0:T(128)S(1)}, f32[128]{0:T(128)}, u32[]{:S(2)}) copy-start(f32[128]{0:T(128)} %param.17) | copy-start | bytes 1540
  77.4 57.0 %all-to-all-start = ((bf16[16,2,32768]{2,1,0:T(2,128)(2,1)}), bf16[16,2,32768]{2,1,0:T(2,128)(2,1)}, u32[]{:S(2)}, u32[]{:S(2)}) async-start(bf16[16,2,32768]{2,1,0:T(2,128)(2,1)} %reshape.136), calls=%async_computation | async-start | bytes 4194304 | tf_op jit(solution)/shard_map/all_to_all | solution.py:89
  86.8 7.8 %copy-start.7 = (f32[128]{0:T(128)S(1)}, f32[128]{0:T(128)}, u32[]{:S(2)}) copy-start(f32[128]{0:T(128)} %param.19) | copy-start | bytes 1540
  86.9 8.7 %copy-start.4 = (f32[4,9216]{1,0:T(4,128)S(1)}, f32[4,9216]{1,0:T(4,128)}, u32[]{:S(2)}) copy-start(f32[4,9216]{1,0:T(4,128)} %param.15) | copy-start | bytes 442372
  159.2 52.4 %all-to-all-start.1 = ((bf16[16,128,512]{2,1,0:T(8,128)(2,1)}), bf16[16,128,512]{2,1,0:T(8,128)(2,1)}, u32[]{:S(2)}, u32[]{:S(2)}) async-start(bf16[16,128,512]{2,1,0:T(8,128)(2,1)} %broadcast_select_fusion), calls=%async_computation.1 | async-start | bytes 4194304 | tf_op jit(solution)/shard_map/all_to_all | solution.py:91
  168.8 1.8 copy-start.5
  182.6 1.3 copy-start.1
  215.8 8.7 %copy-start.2 = (bf16[128,8192]{0,1:T(8,128)(2,1)S(1)}, bf16[128,8192]{0,1:T(8,128)(2,1)}, u32[]{:S(2)}) copy-start(bf16[128,8192]{0,1:T(8,128)(2,1)} %copy-done.1) | copy-start | bytes 6291460
Sparse Core Ops, SparseCore 0:
  10.3 48.3 all-gather.1
where the time goes:
time: 242 us; the launch traced here: 241 us
  other arithmetic  67 us (28%)
  waiting for transfers between devices  60.5 us (25%)
  local copies, waits for them, and re-layouts  55.7 us (23%)
  between operations  19 us (8%)
  matrix products  16.1 us (7%)
  starting transfers between devices  14.4 us (6%)
  blocking collectives  7.91 us (3%)
    unnamed x1, other arithmetic  45.2 us
    unnamed x34, local copies, waits for them, and re-layouts  39.9 us
    all_to_all x1, waiting for transfers between devices, local(): lax.all_to_all(send_states, 'req', split_axis=2, concat_axis=0, tiled=True)  38.7 us
    all_to_all x1, waiting for transfers between devices, local(): lax.all_to_all(state_chosen, 'req', split_axis=0, concat_axis=2, tiled=True)  21.7 us
    convert_element_type x1, other arithmetic, convolve(): return jax.nn.silu(conv).astype(jnp.bfloat16)  11.8 us
    all_to_all x1, starting transfers between devices, local(): lax.all_to_all(send_states, 'req', split_axis=2, concat_axis=0, tiled=True)  9.43 us
    unnamed x1, blocking collectives  7.91 us
    dot_general x1, matrix products, local_part(): jnp.einsum('gjts,sgjp->tgjp', mixing, inputs, preferred_element_type=jnp....  5.99 us
  transfers between devices with their start and end apart: 3, of which 2 were waited for; matrix products, arithmetic and copies ran while one was open for 47% of the time, Pallas kernels for 0%

commit v1 on v0

--- a/solution.py
+++ b/solution.py
@@ -75,6 +75,24 @@
     hit_spans,
     request_of,
 ):
+
+    def _cover_teams(t0, which_axis):
+        r_now, met_up = (lax.axis_size(which_axis), lax.axis_index(which_axis))
+        small = t0.shape[0] // r_now
+        a_now = list(t0.shape)
+        a_now[0] = small
+        current_value = a_now[2]
+        a_now[2] = current_value * r_now
+        b_next = jnp.zeros(a_now, t0.dtype)
+        for it in range(r_now):
+            vec_out = lax.dynamic_slice_in_dim(t0, (met_up ^ it) * small, small, axis=0)
+            if it:
+                vec_out = lax.ppermute(vec_out, which_axis, [(no, no ^ it) for no in range(r_now)])
+            b_next = lax.dynamic_update_slice_in_dim(
+                b_next, vec_out, (met_up ^ it) * current_value, axis=2
+            )
+        return b_next
+
     slots = cache_states.shape[0]
     every_request = lax.all_gather(request_of, "req", axis=0, tiled=True)
     mine = request_of[0]
@@ -88,7 +106,7 @@
     tail = lax.dynamic_index_in_dim(every_tail, own_row, 0, keepdims=False)
     state_parts = lax.all_to_all(send_states, "req", split_axis=2, concat_axis=0, tiled=True)
     state_chosen = jnp.take(state_parts, wanted_rows, axis=0)
-    start = lax.all_to_all(state_chosen, "req", split_axis=0, concat_axis=2, tiled=True)[0]
+    start = _cover_teams(state_chosen, "req")[0]
     tail = jnp.where(live, tail, jnp.zeros_like(tail))
     start = jnp.where(live, start, jnp.zeros_like(start))
     conv_out = convolve(xbc, tail, conv_weight, conv_bias)

time: 242 us -> 305 us (1.26)
  the two profiles are of different devices: /device:TPU:15 before, /device:TPU:25 now
where the time goes in v1:
time: 305 us; the launch traced here: 304 us
  local copies, waits for them, and re-layouts  85.2 us (28%)
  waiting for transfers between devices  81.3 us (27%)
  other arithmetic  65.4 us (21%)
  starting transfers between devices  36.5 us (12%)
  between operations  19.3 us (6%)
  matrix products  9.54 us (3%)
  blocking collectives  6.49 us (2%)
    all_to_all x1, waiting for transfers between devices, local(): lax.all_to_all(send_states, 'req', split_axis=2, concat_axis=0, tiled=True)  58.3 us
    unnamed x1, other arithmetic  45.2 us
    unnamed x80, local copies, waits for them, and re-layouts  34.5 us
    ppermute x15, starting transfers between devices, _cover_teams(): lax.ppermute(vec_out, which_axis, [(no, no ^ it) for no in range(r_now)])  26.2 us
    ppermute x15, waiting for transfers between devices, _cover_teams(): lax.ppermute(vec_out, which_axis, [(no, no ^ it) for no in range(r_now)])  22.5 us
    squeeze x17, local copies, waits for them, and re-layouts, local(): start = _cover_teams(state_chosen, 'req')[0]  17.2 us
    dynamic_update_slice x16, local copies, waits for them, and re-layouts, _cover_teams(): lax.dynamic_update_slice_in_dim(b_next, vec_out, (met_up ^ it) * current_...  15.2 us
    convert_element_type x1, other arithmetic, convolve(): return jax.nn.silu(conv).astype(jnp.bfloat16)  11.8 us
  transfers between devices with their start and end apart: 17, of which 7 were waited for; matrix products, arithmetic and copies ran while one was open for 21% of the time, Pallas kernels for 0%

profile of v1, /device:TPU:25, one launch (start us, length us, event | category | flops | bytes accessed | tf_op | source)
XLA Modules:
  0.0 303.7 jit_solution(8010649839610023202)
XLA Ops:
  7.8 1.2 dynamic-slice
  9.1 0.8 dynamic-update-slice
  9.8 6.5 %all-reduce = s32[16]{0:T(128)S(1)} all-reduce(s32[16]{0:T(128)S(1)} %dynamic-update-slice), channel_id=1, replica_groups=mesh['grp'=2,'req'=16] {'req'}, use_global_device_ids=true, to_apply=%add | all-reduce | flops 16 | bytes 128
  16.3 1.3 compare_select_fusion.3
  19.6 1.7 constant_dynamic-slice_fusion.15
  21.3 6.9 %copy.117 = bf16[1,128,8192]{1,0,2:T(2,128)(2,1)} copy(bf16[1,128,8192]{2,1,0:T(8,128)(2,1)S(1)} %constant_dynamic-slice_fusion.15) | data formatting | bytes 4194304
  28.7 45.2 %reduce.4 = bf16[8192,128]{1,0:T(8,128)(2,1)S(1)} reduce(bf16[8192,1,128]{2,1,0:T(2,128)(2,1)} %bitcast.79, bf16[]{:T(256)} %broadcast.82), dimensions={1}, to_apply=%bitcast.68.reduce_sub_computation | reduce | bytes 4194306
  73.9 2.0 reshape.163
  75.9 10.0 %all-to-all-start = ((bf16[16,2,32768]{2,1,0:T(2,128)(2,1)}), bf16[16,2,32768]{2,1,0:T(2,128)(2,1)S(1)}, u32[]{:S(2)}, u32[]{:S(2)}) async-start(bf16[16,2,32768]{2,1,0:T(2,128)(2,1)} %reshape.163), calls=%async_computation | async-start | bytes 4194304 | tf_op jit(solution)/shard_map/all_to_all | solution.py:107
  88.3 58.3 %all-to-all-done = bf16[16,2,32768]{2,1,0:T(2,128)(2,1)S(1)} async-done(((bf16[16,2,32768]{2,1,0:T(2,128)(2,1)}), bf16[16,2,32768]{2,1,0:T(2,128)(2,1)S(1)}, u32[]{:S(2)}, u32[]{:S(2)}) %all-to-all-start) | async-done | bytes 2097184 | tf_op jit(solution)/shard_map/all_to_all | solution.py:107
  146.5 6.7 %reshape.164 = bf16[8192,1,128]{2,1,0:T(2,128)(2,1)} reshape(bf16[16,2,32768]{2,1,0:T(2,128)(2,1)S(1)} %all-to-all-done) | data formatting | bytes 4194304
  153.2 2.6 copy.116
  155.8 2.6 copy.85
  158.4 2.3 gather_fusion.1
  161.0 0.9 constant_dynamic-slice_fusion
  161.9 7.9 %collective-permute-start.1 = (bf16[1,128,512]{2,1,0:T(8,128)(2,1)S(1)}, bf16[1,128,512]{2,1,0:T(8,128)(2,1)S(1)}, u32[]{:S(2)}, u32[]{:S(2)}) collective-permute-start(bf16[1,128,512]{2,1,0:T(8,128)(2,1)S(1)} %get-tuple-element.25), channel_id=1, source_target_pairs={{0,2},{1,3},{2,0},{3,1},{4,6},{5,7},{6,4},{7,5},{8,10},{9,11},{10,... | collective-permute-start | bytes 393224 | tf_op jit(solution)/shard_map/ppermute | solution.py:90
  170.3 1.7 collective-permute-start.3
  173.1 1.3 collective-permute-start.5
  174.4 1.7 collective-permute-start.6
  176.8 1.2 collective-permute-start.7
  178.0 1.1 collective-permute-start.8
  179.1 2.0 collective-permute-start.9
  181.2 6.7 %collective-permute-done.5 = bf16[1,128,512]{2,1,0:T(8,128)(2,1)S(1)} collective-permute-done((bf16[1,128,512]{2,1,0:T(8,128)(2,1)S(1)}, bf16[1,128,512]{2,1,0:T(8,128)(2,1)S(1)}, u32[]{:S(2)}, u32[]{:S(2)}) %collective-permute-start.5) | collective-permute-done | bytes 131104 | tf_op jit(solution)/shard_map/ppermute | solution.py:90
  187.9 3.0 collective-permute-done.6
  190.9 1.3 collective-permute-start.11
  192.2 2.4 collective-permute-start.12
  194.6 8.2 %collective-permute-done.8 = bf16[1,128,512]{2,1,0:T(8,128)(2,1)S(1)} collective-permute-done((bf16[1,128,512]{2,1,0:T(8,128)(2,1)S(1)}, bf16[1,128,512]{2,1,0:T(8,128)(2,1)S(1)}, u32[]{:S(2)}, u32[]{:S(2)}) %collective-permute-start.8) | collective-permute-done | bytes 131104 | tf_op jit(solution)/shard_map/ppermute | solution.py:90
  202.8 3.8 %collective-permute-done.9 = bf16[1,128,512]{2,1,0:T(8,128)(2,1)S(1)} collective-permute-done((bf16[1,128,512]{2,1,0:T(8,128)(2,1)S(1)}, bf16[1,128,512]{2,1,0:T(8,128)(2,1)S(1)}, u32[]{:S(2)}, u32[]{:S(2)}) %collective-permute-start.9) | collective-permute-done | bytes 131104 | tf_op jit(solution)/shard_map/ppermute | solution.py:90
  206.6 4.9 %collective-permute-start.14 = (bf16[1,128,512]{2,1,0:T(8,128)(2,1)}, bf16[1,128,512]{2,1,0:T(8,128)(2,1)}, u32[]{:S(2)}, u32[]{:S(2)}) collective-permute-start(bf16[1,128,512]{2,1,0:T(8,128)(2,1)} %get-tuple-element.12), channel_id=1, source_target_pairs={{0,15},{1,14},{2,13},{3,12},{4,11},{5,10},{6,9},{7,8},{8,7},{9,6},... | collective-permute-start | bytes 393224 | tf_op jit(solution)/shard_map/ppermute | solution.py:90
  212.8 3.0 %copy.79 = bf16[128,9216]{0,1:T(8,128)(2,1)S(1)} copy(bf16[128,9216]{1,0:T(8,128)(2,1)} %param.13) | data formatting | bytes 4718592 | tf_op args[0]
  217.2 1.3 dynamic_slice.64
  220.6 1.3 mul.182
  222.6 1.2 exp.45
  224.6 1.6 squeeze.45
  226.9 0.8 copy.87
  228.4 0.8 copy.89
  229.2 0.8 copy.90
  229.9 1.6 copy.91
  231.6 1.0 copy.92
  232.6 1.0 copy.93
  233.6 1.0 copy.94
  234.7 1.0 copy.95
  235.7 1.0 copy.96
  236.7 1.0 copy.97
  237.8 1.0 copy.98
  238.8 1.0 copy.99
  239.9 1.0 copy.100
  240.9 1.7 copy.101
  242.6 1.6 constant_dynamic-update-slice_fusion.14
  244.2 1.6 constant_dynamic-update-slice_fusion.13
  245.7 1.6 constant_dynamic-update-slice_fusion.12
  247.3 1.6 constant_dynamic-update-slice_fusion.11
  248.9 1.6 constant_dynamic-update-slice_fusion.10
  257.1 3.0 %broadcast_select_fusion.1 = bf16[128,8192]{0,1:T(8,128)(2,1)} fusion(bf16[128,8192]{0,1:T(8,128)(2,1)} %constant_dynamic-update-slice_fusion, pred[]{:T(512)} %bitcast.2), kind=kLoop, calls=%fused_computation.32 | loop fusion | flops 1048576 | bytes 4194305 | tf_op jit(solution)/shard_map/jit(_where)/select_n | solution.py:111
  260.1 0.9 constant_dynamic-slice_fusion.16
  261.0 2.0 copy.118
  263.0 1.7 select_bitcast_fusion
  264.8 1.8 maximum_convert_fusion
  266.7 11.8 %multiply_convert_fusion.1 = bf16[128,9216]{0,1:T(8,128)(2,1)S(1)} fusion(f32[131,9216]{0,1:T(8,128)S(1)} %maximum_convert_fusion, f32[9216]{0:T(1024)S(1)} %bitcast.98, f32[9216]{0:T(1024)S(1)} %bitcast.99, f32[9216]{0:T(1024)S(1)} %bitcast.97, f32[9216]{0:T(1024)S(1)} %bitcast.96, f32[9216]{0:T(1024)S(1)} %copy-done.28), kind=kLoop, calls=%fused_computation.14 | loop fusion | flops 15335424 | bytes 21417984 | tf_op jit(solution)/shard_map/convert_element_type | solution.py:20
  279.3 3.0 fusion.4
  282.4 2.4 fusion.7
  284.8 4.1 %copy.106 = bf16[128,8192]{1,0:T(8,128)(2,1)} copy(bf16[128,8192]{0,1:T(8,128)(2,1)} %bitcast.88) | data formatting | bytes 4194304
  288.9 3.9 %fusion.9 = bf16[128,4,32,64]{0,3,2,1:T(8,128)(2,1)} fusion(bf16[128,4,32,64]{0,3,2,1:T(8,128)(2,1)S(1)} %bitcast.84, bf16[128,4,128,1]{0,2,3,1:T(8,128)(2,1)S(1)} %bitcast.94, bf16[128,4,32,64]{0,3,2,1:T(8,128)(2,1)} %bitcast.87, f32[128,4,32]{0,2,1:T(8,128)S(1)} %bitcast.110, f32[4,32]{1,0:T(4,128)S(1)} %copy-done.31), kind=kOutput, calls=%fused_computation.21 | convolution fusion | flops 275775488 | bytes 6488576 | tf_op jit(solution)/shard_map/sgn,sgjp->ngjp/dot_general | solution.py:49
  292.8 4.1 %copy.107 = bf16[1,128,8192]{2,1,0:T(8,128)(2,1)} copy(bf16[1,128,8192]{1,2,0:T(8,128)(2,1)} %bitcast.89) | data formatting | bytes 4194304
  (124 shorter events, 18.4 us)
Async XLA Ops:
  75.9 10.8 %copy-start = (s32[16]{0:T(128)S(1)}, s32[16]{0:T(128)}, u32[]{:S(2)}) copy-start(s32[16]{0:T(128)} %param.22) | copy-start | bytes 196
  75.9 11.5 %copy-start.33 = (f32[128]{0:T(128)S(1)}, f32[128]{0:T(128)}, u32[]{:S(2)}) copy-start(f32[128]{0:T(128)} %param.18) | copy-start | bytes 1540
  75.9 11.5 %copy-start.10 = (f32[4,9216]{1,0:T(4,128)S(1)}, f32[4,9216]{1,0:T(4,128)}, u32[]{:S(2)}) copy-start(f32[4,9216]{1,0:T(4,128)} %param.15) | copy-start | bytes 442372
  75.9 70.6 %all-to-all-start = ((bf16[16,2,32768]{2,1,0:T(2,128)(2,1)}), bf16[16,2,32768]{2,1,0:T(2,128)(2,1)S(1)}, u32[]{:S(2)}, u32[]{:S(2)}) async-start(bf16[16,2,32768]{2,1,0:T(2,128)(2,1)} %reshape.163), calls=%async_computation | async-start | bytes 4194304 | tf_op jit(solution)/shard_map/all_to_all | solution.py:107
  85.9 174.2 %all-gather.2.cloned.1.call-start = ((), (), s32[]{:S(2)}) async-start(), calls=%async_computation.1 | async-start | bytes 3760128 | tf_op jit(solution)/shard_map/all_gather | solution.py:105
  161.0 11.4 %copy-start.5 = (f32[128,128]{1,0:T(8,128)S(1)}, f32[128,128]{1,0:T(8,128)}, u32[]{:S(2)}) copy-start(f32[128,128]{1,0:T(8,128)} %param.14) | copy-start | bytes 196612
  161.0 11.3 %copy-start.30 = (f32[128]{0:T(128)S(1)}, f32[128]{0:T(128)}, u32[]{:S(2)}) copy-start(f32[128]{0:T(128)} %param.17) | copy-start | bytes 1540
  161.0 51.1 %copy-start.32 = (s32[16]{0:T(128)S(1)}, s32[16]{0:T(128)}, u32[]{:S(2)}) copy-start(s32[16]{0:T(128)} %param.23) | copy-start | bytes 196
  161.9 11.1 %collective-permute-start = (bf16[1,128,512]{2,1,0:T(8,128)(2,1)S(1)}, bf16[1,128,512]{2,1,0:T(8,128)(2,1)S(1)}, u32[]{:S(2)}, u32[]{:S(2)}) collective-permute-start(bf16[1,128,512]{2,1,0:T(8,128)(2,1)S(1)} %get-tuple-element.26), channel_id=1, source_target_pairs={{0,1},{1,0},{2,3},{3,2},{4,5},{5,4},{6,7},{7,6},{8,9},{9,8},{10,11... | collective-permute-start | bytes 393224 | tf_op jit(solution)/shard_map/ppermute | solution.py:90
  161.9 12.4 %collective-permute-start.1 = (bf16[1,128,512]{2,1,0:T(8,128)(2,1)S(1)}, bf16[1,128,512]{2,1,0:T(8,128)(2,1)S(1)}, u32[]{:S(2)}, u32[]{:S(2)}) collective-permute-start(bf16[1,128,512]{2,1,0:T(8,128)(2,1)S(1)} %get-tuple-element.25), channel_id=1, source_target_pairs={{0,2},{1,3},{2,0},{3,1},{4,6},{5,7},{6,4},{7,5},{8,10},{9,11},{10,... | collective-permute-start | bytes 393224 | tf_op jit(solution)/shard_map/ppermute | solution.py:90
  169.9 6.9 %collective-permute-start.2 = (bf16[1,128,512]{2,1,0:T(8,128)(2,1)S(1)}, bf16[1,128,512]{2,1,0:T(8,128)(2,1)S(1)}, u32[]{:S(2)}, u32[]{:S(2)}) collective-permute-start(bf16[1,128,512]{2,1,0:T(8,128)(2,1)S(1)} %get-tuple-element.24), channel_id=1, source_target_pairs={{0,3},{1,2},{2,1},{3,0},{4,7},{5,6},{6,5},{7,4},{8,11},{9,10},{10,... | collective-permute-start | bytes 393224 | tf_op jit(solution)/shard_map/ppermute | solution.py:90
  170.3 7.6 %collective-permute-start.3 = (bf16[1,128,512]{2,1,0:T(8,128)(2,1)S(1)}, bf16[1,128,512]{2,1,0:T(8,128)(2,1)S(1)}, u32[]{:S(2)}, u32[]{:S(2)}) collective-permute-start(bf16[1,128,512]{2,1,0:T(8,128)(2,1)S(1)} %get-tuple-element.23), channel_id=1, source_target_pairs={{0,4},{1,5},{2,6},{3,7},{4,0},{5,1},{6,2},{7,3},{8,12},{9,13},{10,... | collective-permute-start | bytes 393224 | tf_op jit(solution)/shard_map/ppermute | solution.py:90
  172.0 7.1 %collective-permute-start.4 = (bf16[1,128,512]{2,1,0:T(8,128)(2,1)S(1)}, bf16[1,128,512]{2,1,0:T(8,128)(2,1)S(1)}, u32[]{:S(2)}, u32[]{:S(2)}) collective-permute-start(bf16[1,128,512]{2,1,0:T(8,128)(2,1)S(1)} %get-tuple-element.22), channel_id=1, source_target_pairs={{0,5},{1,4},{2,7},{3,6},{4,1},{5,0},{6,3},{7,2},{8,13},{9,12},{10,... | collective-permute-start | bytes 393224 | tf_op jit(solution)/shard_map/ppermute | solution.py:90
  173.0 39.7 %copy-start.11 = (bf16[1,128,512]{2,1,0:T(8,128)(2,1)}, bf16[1,128,512]{2,1,0:T(8,128)(2,1)S(1)}, u32[]{:S(2)}) copy-start(bf16[1,128,512]{2,1,0:T(8,128)(2,1)S(1)} %collective-permute-done) | copy-start | bytes 393220
  173.1 14.9 %collective-permute-start.5 = (bf16[1,128,512]{2,1,0:T(8,128)(2,1)S(1)}, bf16[1,128,512]{2,1,0:T(8,128)(2,1)S(1)}, u32[]{:S(2)}, u32[]{:S(2)}) collective-permute-start(bf16[1,128,512]{2,1,0:T(8,128)(2,1)S(1)} %get-tuple-element.21), channel_id=1, source_target_pairs={{0,6},{1,7},{2,4},{3,5},{4,2},{5,3},{6,0},{7,1},{8,14},{9,15},{10,... | collective-permute-start | bytes 393224 | tf_op jit(solution)/shard_map/ppermute | solution.py:90
  174.4 38.4 %copy-start.13 = (bf16[1,128,512]{2,1,0:T(8,128)(2,1)}, bf16[1,128,512]{2,1,0:T(8,128)(2,1)S(1)}, u32[]{:S(2)}) copy-start(bf16[1,128,512]{2,1,0:T(8,128)(2,1)S(1)} %collective-permute-done.1) | copy-start | bytes 393220
  174.4 16.5 %collective-permute-start.6 = (bf16[1,128,512]{2,1,0:T(8,128)(2,1)S(1)}, bf16[1,128,512]{2,1,0:T(8,128)(2,1)S(1)}, u32[]{:S(2)}, u32[]{:S(2)}) collective-permute-start(bf16[1,128,512]{2,1,0:T(8,128)(2,1)S(1)} %get-tuple-element.20), channel_id=1, source_target_pairs={{0,7},{1,6},{2,5},{3,4},{4,3},{5,2},{6,1},{7,0},{8,15},{9,14},{10,... | collective-permute-start | bytes 393224 | tf_op jit(solution)/shard_map/ppermute | solution.py:90
  176.8 36.0 %copy-start.15 = (bf16[1,128,512]{2,1,0:T(8,128)(2,1)}, bf16[1,128,512]{2,1,0:T(8,128)(2,1)S(1)}, u32[]{:S(2)}) copy-start(bf16[1,128,512]{2,1,0:T(8,128)(2,1)S(1)} %collective-permute-done.2) | copy-start | bytes 393220
  176.8 15.4 %collective-permute-start.7 = (bf16[1,128,512]{2,1,0:T(8,128)(2,1)S(1)}, bf16[1,128,512]{2,1,0:T(8,128)(2,1)S(1)}, u32[]{:S(2)}, u32[]{:S(2)}) collective-permute-start(bf16[1,128,512]{2,1,0:T(8,128)(2,1)S(1)} %get-tuple-element.19), channel_id=1, source_target_pairs={{0,8},{1,9},{2,10},{3,11},{4,12},{5,13},{6,14},{7,15},{8,0},{9,1},... | collective-permute-start | bytes 393224 | tf_op jit(solution)/shard_map/ppermute | solution.py:90
  177.9 34.8 %copy-start.17 = (bf16[1,128,512]{2,1,0:T(8,128)(2,1)}, bf16[1,128,512]{2,1,0:T(8,128)(2,1)S(1)}, u32[]{:S(2)}) copy-start(bf16[1,128,512]{2,1,0:T(8,128)(2,1)S(1)} %collective-permute-done.3) | copy-start | bytes 393220
  178.0 24.8 %collective-permute-start.8 = (bf16[1,128,512]{2,1,0:T(8,128)(2,1)S(1)}, bf16[1,128,512]{2,1,0:T(8,128)(2,1)S(1)}, u32[]{:S(2)}, u32[]{:S(2)}) collective-permute-start(bf16[1,128,512]{2,1,0:T(8,128)(2,1)S(1)} %get-tuple-element.18), channel_id=1, source_target_pairs={{0,9},{1,8},{2,11},{3,10},{4,13},{5,12},{6,15},{7,14},{8,1},{9,0},... | collective-permute-start | bytes 393224 | tf_op jit(solution)/shard_map/ppermute | solution.py:90
  179.1 33.6 %copy-start.19 = (bf16[1,128,512]{2,1,0:T(8,128)(2,1)}, bf16[1,128,512]{2,1,0:T(8,128)(2,1)S(1)}, u32[]{:S(2)}) copy-start(bf16[1,128,512]{2,1,0:T(8,128)(2,1)S(1)} %collective-permute-done.4) | copy-start | bytes 393220
  179.1 27.5 %collective-permute-start.9 = (bf16[1,128,512]{2,1,0:T(8,128)(2,1)S(1)}, bf16[1,128,512]{2,1,0:T(8,128)(2,1)S(1)}, u32[]{:S(2)}, u32[]{:S(2)}) collective-permute-start(bf16[1,128,512]{2,1,0:T(8,128)(2,1)S(1)} %get-tuple-element.17), channel_id=1, source_target_pairs={{0,10},{1,11},{2,8},{3,9},{4,14},{5,15},{6,12},{7,13},{8,2},{9,3},... | collective-permute-start | bytes 393224 | tf_op jit(solution)/shard_map/ppermute | solution.py:90
  187.9 24.8 %copy-start.20 = (bf16[1,128,512]{2,1,0:T(8,128)(2,1)}, bf16[1,128,512]{2,1,0:T(8,128)(2,1)S(1)}, u32[]{:S(2)}) copy-start(bf16[1,128,512]{2,1,0:T(8,128)(2,1)S(1)} %collective-permute-done.5) | copy-start | bytes 393220
  187.9 48.8 %collective-permute-start.10 = (bf16[1,128,512]{2,1,0:T(8,128)(2,1)}, bf16[1,128,512]{2,1,0:T(8,128)(2,1)}, u32[]{:S(2)}, u32[]{:S(2)}) collective-permute-start(bf16[1,128,512]{2,1,0:T(8,128)(2,1)} %get-tuple-element.16), channel_id=1, source_target_pairs={{0,11},{1,10},{2,9},{3,8},{4,15},{5,14},{6,13},{7,12},{8,3},{9,2},... | collective-permute-start | bytes 393224 | tf_op jit(solution)/shard_map/ppermute | solution.py:90
  190.9 21.8 %copy-start.21 = (bf16[1,128,512]{2,1,0:T(8,128)(2,1)}, bf16[1,128,512]{2,1,0:T(8,128)(2,1)S(1)}, u32[]{:S(2)}) copy-start(bf16[1,128,512]{2,1,0:T(8,128)(2,1)S(1)} %collective-permute-done.6) | copy-start | bytes 393220
  190.9 46.9 %collective-permute-start.11 = (bf16[1,128,512]{2,1,0:T(8,128)(2,1)S(1)}, bf16[1,128,512]{2,1,0:T(8,128)(2,1)}, u32[]{:S(2)}, u32[]{:S(2)}) collective-permute-start(bf16[1,128,512]{2,1,0:T(8,128)(2,1)S(1)} %get-tuple-element.15), channel_id=1, source_target_pairs={{0,12},{1,13},{2,14},{3,15},{4,8},{5,9},{6,10},{7,11},{8,4},{9,5},... | collective-permute-start | bytes 393224 | tf_op jit(solution)/shard_map/ppermute | solution.py:90
  192.2 20.6 %copy-start.22 = (bf16[1,128,512]{2,1,0:T(8,128)(2,1)}, bf16[1,128,512]{2,1,0:T(8,128)(2,1)S(1)}, u32[]{:S(2)}) copy-start(bf16[1,128,512]{2,1,0:T(8,128)(2,1)S(1)} %collective-permute-done.7) | copy-start | bytes 393220
  192.2 46.6 %collective-permute-start.12 = (bf16[1,128,512]{2,1,0:T(8,128)(2,1)S(1)}, bf16[1,128,512]{2,1,0:T(8,128)(2,1)}, u32[]{:S(2)}, u32[]{:S(2)}) collective-permute-start(bf16[1,128,512]{2,1,0:T(8,128)(2,1)S(1)} %get-tuple-element.14), channel_id=1, source_target_pairs={{0,13},{1,12},{2,15},{3,14},{4,9},{5,8},{6,11},{7,10},{8,5},{9,4},... | collective-permute-start | bytes 393224 | tf_op jit(solution)/shard_map/ppermute | solution.py:90
  202.8 10.0 %copy-start.23 = (bf16[1,128,512]{2,1,0:T(8,128)(2,1)}, bf16[1,128,512]{2,1,0:T(8,128)(2,1)S(1)}, u32[]{:S(2)}) copy-start(bf16[1,128,512]{2,1,0:T(8,128)(2,1)S(1)} %collective-permute-done.8) | copy-start | bytes 393220
  202.8 37.1 %collective-permute-start.13 = (bf16[1,128,512]{2,1,0:T(8,128)(2,1)S(1)}, bf16[1,128,512]{2,1,0:T(8,128)(2,1)}, u32[]{:S(2)}, u32[]{:S(2)}) collective-permute-start(bf16[1,128,512]{2,1,0:T(8,128)(2,1)S(1)} %get-tuple-element.13), channel_id=1, source_target_pairs={{0,14},{1,15},{2,12},{3,13},{4,10},{5,11},{6,8},{7,9},{8,6},{9,7},... | collective-permute-start | bytes 393224 | tf_op jit(solution)/shard_map/ppermute | solution.py:90
  206.6 6.2 %copy-start.24 = (bf16[1,128,512]{2,1,0:T(8,128)(2,1)}, bf16[1,128,512]{2,1,0:T(8,128)(2,1)S(1)}, u32[]{:S(2)}) copy-start(bf16[1,128,512]{2,1,0:T(8,128)(2,1)S(1)} %collective-permute-done.9) | copy-start | bytes 393220
  206.6 34.2 %collective-permute-start.14 = (bf16[1,128,512]{2,1,0:T(8,128)(2,1)}, bf16[1,128,512]{2,1,0:T(8,128)(2,1)}, u32[]{:S(2)}, u32[]{:S(2)}) collective-permute-start(bf16[1,128,512]{2,1,0:T(8,128)(2,1)} %get-tuple-element.12), channel_id=1, source_target_pairs={{0,15},{1,14},{2,13},{3,12},{4,11},{5,10},{6,9},{7,8},{8,7},{9,6},... | collective-permute-start | bytes 393224 | tf_op jit(solution)/shard_map/ppermute | solution.py:90
  215.8 11.1 %copy-start.12 = (bf16[1,128,512]{2,1,0:T(8,128)(2,1)S(1)}, bf16[1,128,512]{2,1,0:T(8,128)(2,1)}, u32[]{:S(2)}) copy-start(bf16[1,128,512]{2,1,0:T(8,128)(2,1)} %copy-done.11) | copy-start | bytes 393220
  215.9 11.8 %copy-start.14 = (bf16[1,128,512]{2,1,0:T(8,128)(2,1)S(1)}, bf16[1,128,512]{2,1,0:T(8,128)(2,1)}, u32[]{:S(2)}) copy-start(bf16[1,128,512]{2,1,0:T(8,128)(2,1)} %copy-done.13) | copy-start | bytes 393220
  215.9 12.5 %copy-start.16 = (bf16[1,128,512]{2,1,0:T(8,128)(2,1)S(1)}, bf16[1,128,512]{2,1,0:T(8,128)(2,1)}, u32[]{:S(2)}) copy-start(bf16[1,128,512]{2,1,0:T(8,128)(2,1)} %copy-done.15) | copy-start | bytes 393220
  224.6 4.5 %copy-start.18 = (bf16[1,128,512]{2,1,0:T(8,128)(2,1)S(1)}, bf16[1,128,512]{2,1,0:T(8,128)(2,1)}, u32[]{:S(2)}) copy-start(bf16[1,128,512]{2,1,0:T(8,128)(2,1)} %copy-done.17) | copy-start | bytes 393220
  242.6 13.8 %copy-start.3 = (bf16[128,512]{0,1:T(8,128)(2,1)S(1)}, bf16[128,512]{0,1:T(8,128)(2,1)}, u32[]{:S(2)}) copy-start(bf16[128,512]{0,1:T(8,128)(2,1)} %copy.101) | copy-start | bytes 393220
  264.8 1.9 copy-start.6
  264.8 1.9 copy-start.7
  264.8 1.9 copy-start.8
  264.8 1.9 copy-start.9
  264.8 1.9 copy-start.28
  278.5 0.8 copy-start.26
  278.5 0.9 copy-start.27
  278.6 3.8 %copy-start.2 = (bf16[128,8192]{0,1:T(8,128)(2,1)}, bf16[128,8192]{0,1:T(8,128)(2,1)S(1)}, u32[]{:S(2)}) copy-start(bf16[128,8192]{0,1:T(8,128)(2,1)S(1)} %slice.57) | copy-start | bytes 6291460
  279.3 3.1 %copy-start.1 = (bf16[128,8192]{0,1:T(8,128)(2,1)S(1)}, bf16[128,8192]{0,1:T(8,128)(2,1)}, u32[]{:S(2)}) copy-start(bf16[128,8192]{0,1:T(8,128)(2,1)} %broadcast_select_fusion.1) | copy-start | bytes 6291460
  279.3 3.1 %copy-start.4 = (f32[128,128]{0,1:T(8,128)S(1)}, f32[128,128]{0,1:T(8,128)}, u32[]{:S(2)}) copy-start(f32[128,128]{0,1:T(8,128)} %copy.103) | copy-start | bytes 196612
  279.3 3.1 %copy-start.29 = (f32[4,32]{1,0:T(4,128)S(1)}, f32[4,32]{1,0:T(4,128)}, u32[]{:S(2)}) copy-start(f32[4,32]{1,0:T(4,128)} %mul.182) | copy-start | bytes 1540
  284.8 4.1 %copy-start.25 = (f32[128,128]{0,1:T(8,128)S(1)}, f32[128,128]{0,1:T(8,128)}, u32[]{:S(2)}) copy-start(f32[128,128]{0,1:T(8,128)} %copy.104) | copy-start | bytes 196612
  284.8 4.1 %copy-start.31 = (f32[4,32]{1,0:T(4,128)S(1)}, f32[4,32]{1,0:T(4,128)}, u32[]{:S(2)}) copy-start(f32[4,32]{1,0:T(4,128)} %exp.45) | copy-start | bytes 1540
Sparse Core Ops, SparseCore 0:
  89.0 66.6 all-gather.1
